TPU v7x, 32 devices: a whole 2x2x4 slice. The times are simulated.
32 devices in a mesh: batch: 4 (over x, core), ctx: 4 (over z), head: 2 (over y).
Axes of the slice: x: 2, y: 2, z: 4, core: 2. Of those that a mesh axis runs over, the one named last changes fastest.
Arguments:
- queries: bfloat16 [2, 2048, 1536], P(None, ('batch', 'ctx'), 'head'), parts along dimension 1, may hold values from -6 to 6
- keyvals: bfloat16 [4, 2048, 1536], P(None, ('batch', 'ctx'), 'head'), parts along dimension 1, may hold values from -6 to 6
- w_out: bfloat16 [1536, 3072], P('head'), may hold values from -2.390625 to 2.390625
Outputs:
- output: bfloat16 [2048, 3072], P(('batch', 'ctx'), 'head'), parts along dimension 0
- output_tangent: bfloat16 [2048, 3072], P(('batch', 'ctx'), 'head'), parts along dimension 0
There are 4 independent parts, one for each index of `batch`. A program takes and returns all parts, laid end to end along the dimension named above; an argument that names none is the same for every part. Nothing has to cross between parts.
All inputs are finite; a program needn't handle non-finite values.
Results may differ from a plain program's by a relative error of at most 0.01.
Values may be sent and summed in bfloat16 or wider, within the bound.
A program may use at most 64 MiB of HBM per device.

v0:
```python
import functools
import math

import jax
import jax.numpy as jnp
from jax import lax
from jax.experimental import pallas as pl
from jax.experimental.pallas import tpu as pltpu
from jax.sharding import PartitionSpec as P

HD = 128
RADIUS = 2
AHEAD = 3
LOOK = 2
PIECES = 4
MESH = pl.DeviceIdType.MESH


def kernel(
    sizes, queries, keyvals, w_out, out, out_tan,
    q, kv, w, att, acc, rounded, state,
    q_sem, own_sem, out_sem, w_sem, kv_send, kv_recv, att_send, att_recv,
    wy_send, wy_recv, wb_send, wb_recv,
):
    n_ctx, n_head, n_batch = sizes
    rows = queries.shape[1]
    width = queries.shape[2]
    heads = width // HD
    cols = out.shape[1]
    me = lax.axis_index("ctx")
    mine = lax.axis_index("head")
    b = lax.axis_index("batch")
    bits = [2, 1] if n_batch % 4 == 0 else [1] if n_batch % 2 == 0 else []
    pair = 2 if heads % 2 == 0 else 1
    chunk = pair * HD
    chunks = heads // pair
    piece = chunk // (1 << len(bits))

    def tile_rows(d, r):
        slot = 0 if r == 0 else 2 * r - 1 + d
        return pl.ds(slot * rows, rows)

    def head_cols(h):
        return pl.ds(h * HD, HD)

    def w_rows(group, first, count):
        return pl.ds(pl.multiple_of(group * width + first, piece), count)

    def w_cols(group):
        return pl.ds(pl.multiple_of(group * cols, 128), cols)

    def sign(d):
        return 1 if d == 0 else -1

    def kv_copy(d, r, h):
        to = me + sign(d)
        return pltpu.make_async_remote_copy(
            src_ref=kv.at[h, :, tile_rows(d, r - 1), :],
            dst_ref=kv.at[h, :, tile_rows(d, r), :],
            send_sem=kv_send.at[d, r - 1, h],
            recv_sem=kv_recv.at[d, r - 1, h],
            device_id={"ctx": to},
            device_id_type=MESH,
        )

    def kv_arrival(d, r, h):
        here = kv.at[h, :, tile_rows(d, r), :]
        return pltpu.make_async_remote_copy(
            src_ref=here, dst_ref=here,
            send_sem=kv_send.at[d, r - 1, h],
            recv_sem=kv_recv.at[d, r - 1, h],
            device_id={"ctx": me - sign(d)},
            device_id_type=MESH,
        )

    def sends(d, r):
        if d == 0:
            return (me - (r - 1) >= 0) & (me + 1 < n_ctx)
        return (me + (r - 1) < n_ctx) & (me - 1 >= 0)

    def gets(d, r):
        return me - r >= 0 if d == 0 else me + r < n_ctx

    def kv_start(r, h):
        for d in range(2):
            @pl.when(sends(d, r))
            def _():
                kv_copy(d, r, h).start()

    def kv_wait(r, h):
        for d in range(2):
            @pl.when(gets(d, r))
            def _():
                kv_arrival(d, r, h).wait_recv()

    def bit_of(bit):
        return lax.rem(b // bit, 2)

    def partner(bit):
        return b + bit - 2 * bit * bit_of(bit)

    number = 0
    for place, bit in enumerate(bits):
        number = number + bit_of(bit) * (1 << place)

    def wy_copy(d, c):
        peer = lax.rem(mine + d, n_head)
        return pltpu.make_async_remote_copy(
            src_ref=w_out.at[
                pl.ds(pl.multiple_of(c * chunk + number * piece, piece), piece), w_cols(peer)
            ],
            dst_ref=w.at[w_rows(mine, c * chunk + number * piece, piece), :],
            send_sem=wy_send.at[d - 1, c],
            recv_sem=wy_recv.at[d - 1, c],
            device_id={"head": peer},
            device_id_type=MESH,
        )

    def wy_arrival(d, c):
        sender = lax.rem(mine + n_head - d, n_head)
        here = w.at[w_rows(sender, c * chunk + number * piece, piece), :]
        return pltpu.make_async_remote_copy(
            src_ref=here, dst_ref=here,
            send_sem=wy_send.at[d - 1, c], recv_sem=wy_recv.at[d - 1, c],
            device_id={"head": sender}, device_id_type=MESH,
        )

    def wb_copy(level, d, c, receive=False):
        sender = lax.rem(mine + n_head - d, n_head)
        block = piece << level
        index = number // (1 << level)
        if receive:
            index = index + 1 - 2 * lax.rem(index, 2)
        here = w.at[w_rows(sender, c * chunk + index * block, block), :]
        return pltpu.make_async_remote_copy(
            src_ref=here, dst_ref=here,
            send_sem=wb_send.at[level, d - 1, c], recv_sem=wb_recv.at[level, d - 1, c],
            device_id={"batch": partner(bits[level])}, device_id_type=MESH,
        )

    def w_step(stage, c):
        for d in range(1, n_head):
            if stage == 0:
                wy_arrival(d, c).wait_recv()
                if c + 1 < chunks:
                    wy_copy(d, c + 1).start()
            else:
                wb_copy(stage - 1, d, c, receive=True).wait_recv()
            if stage < len(bits):
                wb_copy(stage, d, c).start()

    def att_copy(d, h):
        return pltpu.make_async_remote_copy(
            src_ref=att.at[mine, h], dst_ref=att.at[mine, h],
            send_sem=att_send.at[d - 1, h], recv_sem=att_recv.at[d - 1, h],
            device_id={"head": lax.rem(mine + d, n_head)}, device_id_type=MESH,
        )

    def att_arrival(d, h):
        sender = lax.rem(mine + n_head - d, n_head)
        return pltpu.make_async_remote_copy(
            src_ref=att.at[sender, h], dst_ref=att.at[sender, h],
            send_sem=att_send.at[d - 1, h], recv_sem=att_recv.at[d - 1, h],
            device_id={"head": sender}, device_id_type=MESH,
        )

    def q_load():
        return pltpu.make_async_copy(queries, q, q_sem)

    def own_load(h):
        return [
            pltpu.make_async_copy(
                keyvals.at[i, :, head_cols(h)],
                kv.at[h, i // 2 + 2 * (i % 2), tile_rows(0, 0), :],
                own_sem.at[h, i],
            )
            for i in range(4)
        ]

    def own_send(h):
        for load in own_load(h):
            load.wait()
        kv_start(1, h)

    def w_load():
        return pltpu.make_async_copy(
            w_out.at[:, w_cols(mine)], w.at[w_rows(mine, 0, width), :], w_sem
        )

    barrier = pltpu.get_barrier_semaphore()
    for d in range(2):
        @pl.when(sends(d, 1))
        def _():
            pl.semaphore_signal(
                barrier, inc=1, device_id={"ctx": me + sign(d)}, device_id_type=MESH
            )
    for d in range(1, n_head):
        pl.semaphore_signal(
            barrier, inc=1, device_id={"head": lax.rem(mine + d, n_head)}, device_id_type=MESH
        )
    for bit in bits:
        pl.semaphore_signal(
            barrier, inc=1, device_id={"batch": partner(bit)}, device_id_type=MESH
        )
    q_load().start()
    for h in range(heads):
        for load in own_load(h):
            load.start()
    w_load().start()
    for d in range(2):
        @pl.when(jnp.logical_not(gets(d, 1)))
        def _():
            kv[:, :, (1 + d) * rows:(2 + d) * rows, :] = jnp.zeros(
                (heads, 4, rows, HD), jnp.bfloat16
            )
    near = jnp.where(me > 0, 1, 0) + jnp.where(me + 1 < n_ctx, 1, 0)
    pl.semaphore_wait(barrier, near + (n_head - 1 + len(bits)))

    for h in range(min(AHEAD, heads)):
        own_send(h)
    for d in range(1, n_head):
        wy_copy(d, 0).start()

    near_rows = 3 * rows
    slot_at = lax.broadcasted_iota(jnp.int32, (1, near_rows), 1) // rows
    visible = (slot_at == 0) | ((slot_at == 1) & gets(0, 1)) | ((slot_at == 2) & gets(1, 1))
    scale = 1.0 / math.sqrt(HD)

    def score(h, at):
        cols_h = slice(h * HD, (h + 1) * HD)
        q_now, q_tan = q[0, :, cols_h], q[1, :, cols_h]
        lhs = jnp.concatenate(
            [
                jnp.concatenate([q_now, jnp.zeros_like(q_now)], axis=1),
                jnp.concatenate([q_tan, q_now], axis=1),
            ],
            axis=0,
        )
        keys = jnp.concatenate([kv[h, 0, at], kv[h, 1, at]], axis=1)
        both = lax.dot_general(
            lhs, keys, (((1,), (1,)), ((), ())), preferred_element_type=jnp.float32
        )
        return both[:rows] * (scale * math.log2(math.e)), both[rows:] * scale

    def mix(h, at, expo, tan_scores):
        weighted = expo * tan_scores
        values = jnp.concatenate([kv[h, 2, at], kv[h, 3, at]], axis=1)
        left = jnp.concatenate([expo.astype(jnp.bfloat16), weighted.astype(jnp.bfloat16)], axis=0)
        mixed = jnp.dot(left, values, preferred_element_type=jnp.float32)
        return (
            jnp.sum(expo, axis=-1, keepdims=True),
            jnp.sum(weighted, axis=-1, keepdims=True),
            mixed[:rows, :HD],
            mixed[rows:, :HD] + mixed[:rows, HD:],
        )

    def attend_near(h):
        at = slice(0, near_rows)
        scores, tan_scores = score(h, at)
        scores = jnp.where(visible, scores, -jnp.inf)
        row_max = jnp.max(scores, axis=-1, keepdims=True)
        parts = mix(h, at, jnp.exp2(scores - row_max), tan_scores)
        for i, part in enumerate((row_max,) + parts):
            state[h, i] = jnp.broadcast_to(part, (rows, HD))

    def attend_far(h, d, r):
        slot = 2 * r - 1 + d
        at = slice(slot * rows, (slot + 1) * rows)
        scores, tan_scores = score(h, at)
        old_max = state[h, 0]
        row_max = jnp.maximum(old_max, jnp.max(scores, axis=-1, keepdims=True))
        shrink = jnp.exp2(old_max - row_max)
        parts = mix(h, at, jnp.exp2(scores - row_max[:, :1]), tan_scores)
        state[h, 0] = row_max
        for i, part in enumerate(parts):
            state[h, 1 + i] = state[h, 1 + i] * shrink + part

    def attend(h):
        for r in range(2, RADIUS + 1):
            for d in range(2):
                @pl.when(gets(d, r))
                def _():
                    kv_arrival(d, r, h).wait_recv()
                    attend_far(h, d, r)
        inverse = 1.0 / state[h, 1]
        attended = state[h, 3] * inverse
        tangent = state[h, 4] * inverse - (state[h, 2] * inverse) * attended
        att[mine, h, :rows] = attended.astype(jnp.bfloat16)
        att[mine, h, rows:] = tangent.astype(jnp.bfloat16)
        for d in range(1, n_head):
            att_copy(d, h).start()

    block = 512 if cols % 512 == 0 else cols

    def out_copies(i):
        at = pl.ds(i * block, block)
        return [
            pltpu.make_async_copy(rounded.at[pl.ds(n * rows, rows), at], to.at[:, at], out_sem.at[n, i])
            for n, to in enumerate((out, out_tan))
        ]

    def finish(group, first, count):
        left = jnp.concatenate([att[group, first + i] for i in range(count)], axis=1)
        for i in range(cols // block):
            at = slice(i * block, (i + 1) * block)
            part = jnp.dot(
                left, w[w_rows(group, first * HD, count * HD), at],
                preferred_element_type=jnp.float32,
            )
            rounded[:, at] = (acc[:, at] + part).astype(rounded.dtype)
            for copy in out_copies(i):
                copy.start()

    def project(group, first, count, fresh=False):
        left = jnp.concatenate([att[group, first + i] for i in range(count)], axis=1)
        part = jnp.dot(
            left, w[w_rows(group, first * HD, count * HD), :], preferred_element_type=jnp.float32
        )
        if fresh:
            acc[...] = part
        else:
            acc[...] += part

    def near_step(h):
        kv_wait(1, h)
        kv_start(2, h)
        if h + AHEAD < heads:
            own_send(h + AHEAD)

    def project_far(c):
        for d in range(1, n_head):
            for i in range(pair):
                att_arrival(d, c * pair + i).wait_recv()
            last = c == chunks - 1 and d == n_head - 1
            (finish if last else project)(lax.rem(mine + n_head - d, n_head), c * pair, pair)

    arrived = 0
    projected = 0

    def w_steps(step):
        done = 0
        for stage in range(len(bits) + 1):
            if 0 <= step - stage < chunks:
                w_step(stage, step - stage)
                done += stage == len(bits)
        return done

    q_load().wait()
    near_step(0)
    attend_near(0)
    for h in range(1, min(LOOK, heads)):
        near_step(h)
    for h in range(heads):
        if h + LOOK < heads:
            near_step(h + LOOK)
        if h + 1 < heads:
            attend_near(h + 1)
        if h == 1:
            w_load().wait()
        if h > 0:
            arrived += w_steps(h - 1)
            if h % pair == 0:
                project(mine, h - pair, pair, fresh=h == pair)
            if projected < arrived and (projected + 1) * pair < h:
                project_far(projected)
                projected += 1
        attend(h)
    project(mine, heads - pair, pair, fresh=heads == pair)
    arrived += w_steps(heads - 1)
    for step in range(heads, chunks + len(bits)):
        arrived += w_steps(step)
    for c in range(projected, chunks):
        project_far(c)
    for h in range(heads):
        for r in range(1, RADIUS + 1):
            for d in range(2):
                @pl.when(sends(d, r))
                def _():
                    kv_copy(d, r, h).wait_send()
        for d in range(1, n_head):
            att_copy(d, h).wait_send()
    for d in range(1, n_head):
        for c in range(chunks):
            wy_copy(d, c).wait_send()
            for level in range(len(bits)):
                wb_copy(level, d, c).wait_send()
    for i in range(cols // block):
        for copy in out_copies(i):
            copy.wait()


def place(results, results_tan, out, out_tan, held, in_sem, out_sem):
    rows = out.shape[0] // PIECES
    loads, stores = [], []
    for i in range(PIECES):
        at = pl.ds(i * rows, rows)
        for n, (src, dst) in enumerate(((results, out), (results_tan, out_tan))):
            loads.append(pltpu.make_async_copy(src.at[at], held.at[n, at], in_sem.at[n, i]))
            stores.append(pltpu.make_async_copy(held.at[n, at], dst.at[at], out_sem.at[n, i]))
    for load in loads:
        load.start()
    for load, store in zip(loads, stores):
        load.wait()
        store.start()
    for store in stores:
        store.wait()


def per_device(sizes, queries, keyvals, w_out):
    n_ctx, n_head, n_batch = sizes
    rows, width = queries.shape[1], queries.shape[2]
    heads = width // HD
    cols = w_out.shape[1] // n_head
    slots = 2 * RADIUS + 1
    dma = pltpu.SemaphoreType.DMA
    peers = max(n_head - 1, 1)
    results = pl.pallas_call(
        functools.partial(kernel, sizes),
        out_shape=[jax.ShapeDtypeStruct((rows, cols), jnp.bfloat16)] * 2,
        in_specs=[pl.BlockSpec(memory_space=pl.ANY)] * 3,
        out_specs=[pl.BlockSpec(memory_space=pl.ANY)] * 2,
        scratch_shapes=[
            pltpu.VMEM((2, rows, width), jnp.bfloat16),
            pltpu.VMEM((heads, 4, slots * rows, HD), jnp.bfloat16),
            pltpu.VMEM((n_head * width, cols), jnp.bfloat16),
            pltpu.VMEM((n_head, heads, 2 * rows, HD), jnp.bfloat16),
            pltpu.VMEM((2 * rows, cols), jnp.float32),
            pltpu.VMEM((2 * rows, cols), jnp.bfloat16),
            pltpu.VMEM((heads, 5, rows, HD), jnp.float32),
            dma, dma((heads, 4)), dma((2, cols // HD)), dma,
            dma((2, RADIUS, heads)), dma((2, RADIUS, heads)),
            dma((peers, heads)), dma((peers, heads)),
            dma((peers, heads)), dma((peers, heads)),
            dma((2, peers, heads)), dma((2, peers, heads)),
        ],
        compiler_params=pltpu.CompilerParams(
            collective_id=0, has_side_effects=True, vmem_limit_bytes=63 * 1024 * 1024
        ),
        cost_estimate=pl.CostEstimate(
            flops=2 * 2 * rows * n_head * width * cols,
            bytes_accessed=16 * rows * width + 2 * w_out.size,
            transcendentals=heads * rows * slots * rows,
        ),
    )(queries, keyvals, w_out)
    return pl.pallas_call(
        place,
        out_shape=[jax.ShapeDtypeStruct((rows, cols), jnp.bfloat16)] * 2,
        in_specs=[pl.BlockSpec(memory_space=pl.ANY)] * 2,
        out_specs=[pl.BlockSpec(memory_space=pl.ANY)] * 2,
        scratch_shapes=[
            pltpu.VMEM((2, rows, cols), jnp.bfloat16), dma((2, PIECES)), dma((2, PIECES)),
        ],
        compiler_params=pltpu.CompilerParams(vmem_limit_bytes=63 * 1024 * 1024),
    )(*results)


def solution(mesh):
    sizes = (mesh.shape["ctx"], mesh.shape["head"], mesh.shape["batch"])
    in_specs = (
        P(None, ("batch", "ctx"), "head"),
        P(None, ("batch", "ctx"), "head"),
        P("head", None),
    )
    out_specs = (P(("batch", "ctx"), "head"), P(("batch", "ctx"), "head"))
    return jax.shard_map(
        functools.partial(per_device, sizes),
        mesh=mesh, in_specs=in_specs, out_specs=out_specs, check_vma=False,
    )
```

profile of v0, /device:TPU:0, one launch (start us, length us, event | category | flops | bytes accessed | tf_op | source)
XLA Modules:
  0.0 48.6 jit_solution(3649670457643796403)
XLA Ops:
  0.6 46.0 %shard_map.50 = (bf16[128,1536]{1,0:T(8,128)(2,1)}, bf16[128,1536]{1,0:T(8,128)(2,1)}) custom-call(bf16[2,128,768]{2,1,0:T(8,128)(2,1)} %queries.1, bf16[4,128,768]{2,1,0:T(8,128)(2,1)} %keyvals.1, bf16[768,3072]{1,0:T(8,128)(2,1)} %w_out.1), custom_call_target="tpu_custom_call" | custom-call | flops 1207959552 | bytes 6291456 | tf_op jit(solution)/shard_map/pallas_call | solution.py:417
  46.6 2.0 %shard_map.51 = (bf16[128,1536]{1,0:T(8,128)(2,1)}, bf16[128,1536]{1,0:T(8,128)(2,1)}) custom-call(bf16[128,1536]{1,0:T(8,128)(2,1)} %get-tuple-element.4.results, bf16[128,1536]{1,0:T(8,128)(2,1)} %get-tuple-element.5.results_tan), custom_call_target="tpu_custom_call" | custom-call | tf_op jit(solution)/shard_map/pallas_call | solution.py:445
where the time goes:
time: 48.8 us; the launch traced here: 48.6 us
  Pallas kernels  48 us (98%)
  between operations  0.64 us (1%)
    pallas_call x1, Pallas kernels, per_device(): pl.pallas_call(functools.partial(kernel, sizes), out_shape=[jax.ShapeDtyp...  46 us
    pallas_call x1, Pallas kernels, per_device(): pl.pallas_call(place, out_shape=[jax.ShapeDtypeStruct((rows, cols), jnp.b...  1.99 us

commit v1 on v0

--- a/solution.py
+++ b/solution.py
@@ -142,8 +142,8 @@
         for d in range(1, n_head):
             if stage == 0:
                 wy_arrival(d, c).wait_recv()
-                if c + 1 < chunks:
-                    wy_copy(d, c + 1).start()
+                if c + 2 < chunks:
+                    wy_copy(d, c + 2).start()
             else:
                 wb_copy(stage - 1, d, c, receive=True).wait_recv()
             if stage < len(bits):
@@ -219,7 +219,8 @@
     for h in range(min(AHEAD, heads)):
         own_send(h)
     for d in range(1, n_head):
-        wy_copy(d, 0).start()
+        for c in range(min(2, chunks)):
+            wy_copy(d, c).start()
 
     near_rows = 3 * rows
     slot_at = lax.broadcasted_iota(jnp.int32, (1, near_rows), 1) // rows
@@ -340,8 +341,9 @@
     def w_steps(step):
         done = 0
         for stage in range(len(bits) + 1):
-            if 0 <= step - stage < chunks:
-                w_step(stage, step - stage)
+            c = step - stage - (stage > 0)
+            if 0 <= c < chunks:
+                w_step(stage, c)
                 done += stage == len(bits)
         return done
 
@@ -357,8 +359,8 @@
             attend_near(h + 1)
         if h == 1:
             w_load().wait()
+        arrived += w_steps(h)
         if h > 0:
-            arrived += w_steps(h - 1)
             if h % pair == 0:
                 project(mine, h - pair, pair, fresh=h == pair)
             if projected < arrived and (projected + 1) * pair < h:
@@ -366,8 +368,7 @@
                 projected += 1
         attend(h)
     project(mine, heads - pair, pair, fresh=heads == pair)
-    arrived += w_steps(heads - 1)
-    for step in range(heads, chunks + len(bits)):
+    for step in range(heads, chunks + len(bits) + 1):
         arrived += w_steps(step)
     for c in range(projected, chunks):
         project_far(c)

time: 48.8 us -> 48.3 us (0.990)
  Pallas kernels: 48 us -> 47.5 us
    pallas_call x1, Pallas kernels: 46 us -> 45.5 us  [per_device(): pl.pallas_call(functools.partial(kernel, sizes), out_shape=[jax.ShapeDtyp...]
where the time goes in v1:
time: 48.3 us; the launch traced here: 48.1 us
  Pallas kernels  47.5 us (98%)
  between operations  0.64 us (1%)
    pallas_call x1, Pallas kernels, per_device(): pl.pallas_call(functools.partial(kernel, sizes), out_shape=[jax.ShapeDtyp...  45.5 us
    pallas_call x1, Pallas kernels, per_device(): pl.pallas_call(place, out_shape=[jax.ShapeDtypeStruct((rows, cols), jnp.b...  1.99 us

profile of v1, /device:TPU:0, one launch (start us, length us, event | category | flops | bytes accessed | tf_op | source)
XLA Modules:
  0.0 48.1 jit_solution(9587695040221389892)
XLA Ops:
  0.6 45.5 %shard_map.50 = (bf16[128,1536]{1,0:T(8,128)(2,1)}, bf16[128,1536]{1,0:T(8,128)(2,1)}) custom-call(bf16[2,128,768]{2,1,0:T(8,128)(2,1)} %queries.1, bf16[4,128,768]{2,1,0:T(8,128)(2,1)} %keyvals.1, bf16[768,3072]{1,0:T(8,128)(2,1)} %w_out.1), custom_call_target="tpu_custom_call" | custom-call | flops 1207959552 | bytes 6291456 | tf_op jit(solution)/shard_map/pallas_call | solution.py:418
  46.1 2.0 %shard_map.51 = (bf16[128,1536]{1,0:T(8,128)(2,1)}, bf16[128,1536]{1,0:T(8,128)(2,1)}) custom-call(bf16[128,1536]{1,0:T(8,128)(2,1)} %get-tuple-element.4.results, bf16[128,1536]{1,0:T(8,128)(2,1)} %get-tuple-element.5.results_tan), custom_call_target="tpu_custom_call" | custom-call | tf_op jit(solution)/shard_map/pallas_call | solution.py:446

commit v2 on v1

--- a/solution.py
+++ b/solution.py
@@ -10,7 +10,7 @@
 
 HD = 128
 RADIUS = 2
-AHEAD = 3
+AHEAD = 2
 LOOK = 2
 PIECES = 4
 MESH = pl.DeviceIdType.MESH
@@ -87,6 +87,12 @@
             def _():
                 kv_copy(d, r, h).start()
 
+    def kv_sent(r, h):
+        for d in range(2):
+            @pl.when(sends(d, r))
+            def _():
+                kv_copy(d, r, h).wait_send()
+
     def kv_wait(r, h):
         for d in range(2):
             @pl.when(gets(d, r))
@@ -323,10 +329,11 @@
             acc[...] += part
 
     def near_step(h):
+        if h + AHEAD < heads:
+            kv_sent(1, h)
+            own_send(h + AHEAD)
         kv_wait(1, h)
         kv_start(2, h)
-        if h + AHEAD < heads:
-            own_send(h + AHEAD)
 
     def project_far(c):
         for d in range(1, n_head):
@@ -374,10 +381,8 @@
         project_far(c)
     for h in range(heads):
         for r in range(1, RADIUS + 1):
-            for d in range(2):
-                @pl.when(sends(d, r))
-                def _():
-                    kv_copy(d, r, h).wait_send()
+            if r > 1 or h + AHEAD >= heads:
+                kv_sent(r, h)
         for d in range(1, n_head):
             att_copy(d, h).wait_send()
     for d in range(1, n_head):

time: 48.3 us -> 48.3 us (level)
  no operation moved by 1% of the time
where the time goes in v2:
time: 48.3 us; the launch traced here: 48.1 us
  Pallas kernels  47.5 us (98%)
  between operations  0.64 us (1%)
    pallas_call x1, Pallas kernels, per_device(): pl.pallas_call(functools.partial(kernel, sizes), out_shape=[jax.ShapeDtyp...  45.5 us
    pallas_call x1, Pallas kernels, per_device(): pl.pallas_call(place, out_shape=[jax.ShapeDtypeStruct((rows, cols), jnp.b...  1.99 us

profile of v2, /device:TPU:0, one launch (start us, length us, event | category | flops | bytes accessed | tf_op | source)
XLA Modules:
  0.0 48.1 jit_solution(650301612267005127)
XLA Ops:
  0.6 45.5 %shard_map.50 = (bf16[128,1536]{1,0:T(8,128)(2,1)}, bf16[128,1536]{1,0:T(8,128)(2,1)}) custom-call(bf16[2,128,768]{2,1,0:T(8,128)(2,1)} %queries.1, bf16[4,128,768]{2,1,0:T(8,128)(2,1)} %keyvals.1, bf16[768,3072]{1,0:T(8,128)(2,1)} %w_out.1), custom_call_target="tpu_custom_call" | custom-call | flops 1207959552 | bytes 6291456 | tf_op jit(solution)/shard_map/pallas_call | solution.py:423
  46.1 2.0 %shard_map.51 = (bf16[128,1536]{1,0:T(8,128)(2,1)}, bf16[128,1536]{1,0:T(8,128)(2,1)}) custom-call(bf16[128,1536]{1,0:T(8,128)(2,1)} %get-tuple-element.4.results, bf16[128,1536]{1,0:T(8,128)(2,1)} %get-tuple-element.5.results_tan), custom_call_target="tpu_custom_call" | custom-call | tf_op jit(solution)/shard_map/pallas_call | solution.py:451
